TPU v7x, 32 devices: a whole 2x2x4 slice. The times are simulated.
32 devices in a mesh: sec: 4 (over y, core), mom: 2 (over x), en: 4 (over z).
Axes of the slice: x: 2, y: 2, z: 4, core: 2. Of those that a mesh axis runs over, the one named last changes fastest.
Arguments:
- green_blocks: bfloat16 [2, 32, 2, 128, 128], P('mom', ('sec', 'en')), may hold values from -6 to 6
- derivative: bfloat16 [3, 128, 128], replicated, may hold values from -0.5 to 0.5
- bare_phonon: float32 [4, 2, 2, 3, 3, 128], P('sec', 'mom'), may hold values from -4 to 4
- prior_polar: float32 [4, 2, 2, 3, 3, 128], P('sec', 'mom'), may hold values from -4 to 4
- offsets: int32 [4], replicated, may hold values from 1 to 2, as said below
- momenta: int32 [2, 2], replicated, may hold values from 0 to 1, as said below
Outputs:
- sigma: float32 [2, 32, 2, 128, 128], P('mom', ('sec', 'en'))
- polarization: float32 [4, 2, 3, 128], P('sec', 'mom')
Inputs may be any that keep to these rules, and one draw needn't show every extreme that they name: `offsets`: every mode's offset lies in 1 to 2; some mode's offset equals 2 and another mode's equals 1. momenta[k, k'] = p((k - k') mod 2) for a permutation p of the 2 phonon momenta.
All inputs are finite; a program needn't handle non-finite values.
Results may differ from a plain program's by a relative error of at most 0.014.
Values may be sent and summed in bfloat16 or wider, within the bound.
A program may use at most 64 MiB of HBM per device.

v0:
```python
import math

import jax
import jax.numpy as jnp
from jax import lax
from jax.sharding import PartitionSpec as P


def passed_along(x, axis, by):
    peers = lax.axis_size(axis)
    pairs = [(i, i + by) for i in range(peers) if 0 <= i + by < peers]
    return lax.ppermute(x, axis, pairs)


def contract(former, latter):
    return jnp.sum(former[..., :, :, None, :] * latter[..., None, :, :, :], axis=-3)


def complex_product(former, latter):
    real_part = contract(former[..., 0, :, :, :], latter[..., 0, :, :, :]) - contract(
        former[..., 1, :, :, :], latter[..., 1, :, :, :]
    )
    imag_part = contract(former[..., 0, :, :, :], latter[..., 1, :, :, :]) + contract(
        former[..., 1, :, :, :], latter[..., 0, :, :, :]
    )
    return jnp.stack([real_part, imag_part], axis=-4)


def dyson_update(bare_phonon, prior_polar):
    return bare_phonon + complex_product(complex_product(bare_phonon, prior_polar), bare_phonon)


def flipped_products(blocks, derivative):
    flipped = jnp.einsum(
        "ktcbx,ixa->kticab", blocks, derivative, preferred_element_type=jnp.float32
    )
    sign_flip = jnp.array([1.0, -1.0], jnp.float32).reshape(1, 1, 1, 2, 1, 1)
    return (flipped * sign_flip).astype(jnp.bfloat16)


def mode_weights(chosen):
    real_part = chosen[:, :, 0]
    imag_part = chosen[:, :, 1]
    upper_part = jnp.stack([real_part, -imag_part], axis=2)
    lower_part = jnp.stack([imag_part, real_part], axis=2)
    return jnp.stack([upper_part, lower_part], axis=2)


def weighted_rows(weights, selected):
    mode_count = weights.shape[1]
    total = None
    for mode_index in range(mode_count):
        for part_index in range(2):
            for direction in range(3):
                factor = jnp.transpose(
                    weights[:, mode_index, :, part_index, direction, :, :], (0, 2, 1, 3)
                )
                slab = selected[direction, :, mode_index, part_index].astype(jnp.float32)
                term = factor[:, None, :, :, :, None] * slab[None, :, None, None, :, :]
                total = term if total is None else total + term
    return total.astype(jnp.bfloat16)


def point_terms(source, chosen, derivative, offsets, targets, levels, flipped):
    blocks = jnp.einsum(
        "iab,scbd->iscad", derivative, source, preferred_element_type=jnp.float32
    ).astype(jnp.bfloat16)
    mode_count = chosen.shape[1]
    selected = jnp.stack(
        [
            lax.dynamic_slice_in_dim(blocks, levels - offsets[mode_index], targets, 1)
            for mode_index in range(mode_count)
        ],
        axis=2,
    )
    weights = mode_weights(chosen)
    combined = weighted_rows(weights, selected)
    sigma_part = jnp.einsum(
        "ktjxab,jbd->ktxad", combined, derivative, preferred_element_type=jnp.float32
    )
    polar_part = jnp.einsum(
        "itmcab,kticab->kmia", selected, flipped, preferred_element_type=jnp.float32
    )
    return (sigma_part, polar_part)


def per_device(green_blocks, derivative, bare_phonon, prior_polar, offsets, momenta):
    points = green_blocks.shape[0]
    levels = green_blocks.shape[1]
    block_order = green_blocks.shape[-1]
    all_points = points * lax.axis_size("mom")
    all_levels = levels * lax.axis_size("sec") * lax.axis_size("en")
    phonon = dyson_update(bare_phonon, prior_polar)
    local_modes = phonon.shape[0]
    stacked = phonon.reshape((local_modes * points,) + phonon.shape[2:])
    gathered = lax.all_gather(stacked, ("sec", "mom"), axis=0, tiled=True)
    mode_count = gathered.shape[0] // all_points
    phonon_table = jnp.transpose(
        gathered.reshape((mode_count, all_points) + phonon.shape[2:]), (1, 0, 2, 3, 4, 5)
    )
    own_rows = lax.dynamic_slice_in_dim(momenta, lax.axis_index("mom") * points, points, 0)
    momentum_ids = lax.broadcasted_iota(jnp.int32, (points, all_points), 1)
    lower_rim = passed_along(green_blocks, ("sec", "en"), 1)
    travelling = jnp.concatenate([lower_rim, green_blocks], axis=1)
    targets = green_blocks.shape[1]
    flipped = flipped_products(green_blocks, derivative)
    initial = (
        jnp.zeros((points, targets, 2, block_order, block_order), jnp.float32),
        jnp.zeros((all_points, mode_count, 3, block_order), jnp.float32),
    )
    pieces = lax.all_gather(travelling, "mom", axis=0, tiled=True)

    def one_point(position, running):
        sigma_sum, polar_sum = running
        source = lax.dynamic_index_in_dim(pieces, position, 0, keepdims=False)
        column = lax.dynamic_index_in_dim(own_rows, position, 1, keepdims=False)
        onehot = (column[:, None] == momentum_ids).astype(jnp.float32)
        chosen = jnp.einsum(
            "kq,qmxija->kmxija", onehot, phonon_table, precision=lax.Precision.HIGHEST
        )
        sigma_part, polar_part = point_terms(
            source, chosen, derivative, offsets, targets, levels, flipped
        )
        polar_sum = polar_sum + jnp.einsum(
            "kq,kmia->qmia", onehot, polar_part, precision=lax.Precision.HIGHEST
        )
        return (sigma_sum + sigma_part, polar_sum)

    sigma_sum, polar_sum = lax.fori_loop(0, pieces.shape[0], one_point, initial)
    sigma_scale = 1.0 / math.sqrt(9.0 * mode_count * all_points)
    polar_scale = 1.0 / math.sqrt(float(all_points * all_levels * block_order))
    ordered = jnp.transpose(polar_sum, (1, 0, 2, 3))
    shares = lax.psum_scatter(
        ordered.reshape(mode_count * all_points, 3, block_order).astype(jnp.bfloat16),
        ("sec", "mom"),
        scatter_dimension=0,
        tiled=True,
    ).astype(jnp.float32)
    own_share = lax.psum(shares, "en").reshape(local_modes, points, 3, block_order)
    return (sigma_sum * sigma_scale, own_share * polar_scale)


def solution(mesh):
    return jax.shard_map(
        per_device,
        mesh=mesh,
        in_specs=(
            P("mom", ("sec", "en"), None, None, None),
            P(),
            P("sec", "mom", None, None, None, None),
            P("sec", "mom", None, None, None, None),
            P(),
            P(),
        ),
        out_specs=(P("mom", ("sec", "en"), None, None, None), P("sec", "mom", None, None)),
        check_vma=False,
    )
```

profile of v0, /device:TPU:0, one launch (start us, length us, event | category | flops | bytes accessed | tf_op | source)
XLA Modules:
  0.0 127.5 jit_solution(10402939566199544955)
XLA Ops:
  0.7 4.9 %collective-permute-start = (bf16[1,2,2,128,128]{4,3,2,1,0:T(8,128)(2,1)}, bf16[1,2,2,128,128]{4,3,2,1,0:T(8,128)(2,1)S(1)}, u32[]{:S(2)}, u32[]{:S(2)}) collective-permute-start(bf16[1,2,2,128,128]{4,3,2,1,0:T(8,128)(2,1)} %param.9), channel_id=1, source_target_pairs={{0,1},{1,2},{2,3},{3,8},{8,9},{9,10},{10,11},{11,16},{16,17},{17,1... | collective-permute-start | bytes 393224 | tf_op jit(solution)/shard_map/ppermute | solution.py:12
  5.6 0.8 fusion.139
  6.4 0.8 fusion.140
  8.1 1.2 fusion.135
  15.3 15.9 %all-gather = f32[8,1,2,3,3,128]{5,2,4,3,1,0:T(2,128)S(1)} all-gather(f32[1,1,2,3,3,128]{5,2,4,3,1,0:T(2,128)S(1)} %copy.132), channel_id=2, replica_groups=mesh['sec'=4,'mom'=2,'en'=4] {'sec','mom'}, dimensions={0}, use_global_device_ids=true | all-gather | bytes 82944 | tf_op jit(solution)/shard_map/all_gather | solution.py:96
  33.1 9.8 %all_gather.7 = bf16[2,4,2,128,128]{4,3,2,1,0:T(8,128)(2,1)S(1)} all-gather(bf16[1,4,2,128,128]{4,3,2,1,0:T(8,128)(2,1)S(1)} %pad_maximum_fusion.1), channel_id=1, replica_groups=mesh['sec'=4,'mom'=2,'en'=4] {'mom'}, dimensions={0}, use_global_device_ids=true | all-gather | bytes 786432 | tf_op jit(solution)/shard_map/all_gather | solution.py:111
  42.9 58.0 %while.19 = (s32[]{:T(128)}, f32[1,2,2,128,128]{4,3,2,1,0:T(8,128)}, f32[2,4,3,128]{3,2,1,0:T(4,128)S(1)}, s32[1,2]{1,0:T(1,128)}, f32[2,4,2,3,3,128]{5,4,3,2,1,...) while((s32[]{:T(128)}, ...), condition=%wide.region_9.10_spmd.clone, body=%wide.region_8.9_spmd.clone.sunk | while | flops 166928384 | bytes 31285848 | solution.py:129
  43.0 1.3 constant_dynamic-slice_fusion.3
  44.2 1.2 bitcast_convert_fusion.5
  45.4 1.8 %fusion.161 = f32[1,4,2,3,3,128]{5,0,4,3,2,1:T(1,128)S(1)} fusion(f32[2,4,2,3,3,128]{5,4,3,2,1,0:T(4,128)} %get-tuple-element.754, s32[]{:T(128)} %bitcast.409), kind=kOutput, calls=%fused_computation.110.clone.1 | convolution fusion | flops 221186 | bytes 110596 | tf_op jit(solution)/shard_map/while/body/eval_jaxpr/kq,qmxija->kmxija/dot_general | solution.py:118
  50.5 0.8 copy.218
  52.7 0.8 copy.221
  55.0 0.8 copy.224
  64.9 6.9 %fusion.167 = f32[1,2,2,128,128]{4,3,2,1,0:T(8,128)} fusion(f32[2,128,128]{2,1,0:T(8,128)S(1)} %copy-done.13, f32[3,2,128]{2,0,1:T(4,128)S(1)} %get-tuple-element.673, f32[2,128,128]{2,1,0:T(8,128)} %copy.206, f32[3,2,128]{2,0,1:T(4,128)S(1)} %get-tuple-element.675, f32[2,128,128]{2,1,0:T(8,128)} %copy.207, f32[3,2,128]{2,0,1:T(4,128)S(1)} %get-tuple-element.677, ...), kind=kOutput, calls=%fused_computation.5.clone.1 | convolution fusion | flops 59899904 | bytes 3842049 | tf_op jit(solution)/shard_map/while/body/eval_jaxpr/ktjxab,jbd->ktxad/dot_general | solution.py:78
  71.8 1.3 constant_dynamic-slice_fusion.3
  73.1 1.2 bitcast_convert_fusion.5
  74.3 1.8 %fusion.161 = f32[1,4,2,3,3,128]{5,0,4,3,2,1:T(1,128)S(1)} fusion(f32[2,4,2,3,3,128]{5,4,3,2,1,0:T(4,128)} %get-tuple-element.754, s32[]{:T(128)} %bitcast.409), kind=kOutput, calls=%fused_computation.110.clone.1 | convolution fusion | flops 221186 | bytes 110596 | tf_op jit(solution)/shard_map/while/body/eval_jaxpr/kq,qmxija->kmxija/dot_general | solution.py:118
  79.4 0.8 copy.218
  81.6 0.8 copy.221
  83.9 0.8 copy.224
  93.8 7.1 %fusion.167 = f32[1,2,2,128,128]{4,3,2,1,0:T(8,128)} fusion(f32[2,128,128]{2,1,0:T(8,128)S(1)} %copy-done.13, f32[3,2,128]{2,0,1:T(4,128)S(1)} %get-tuple-element.673, f32[2,128,128]{2,1,0:T(8,128)} %copy.206, f32[3,2,128]{2,0,1:T(4,128)S(1)} %get-tuple-element.675, f32[2,128,128]{2,1,0:T(8,128)} %copy.207, f32[3,2,128]{2,0,1:T(4,128)S(1)} %get-tuple-element.677, ...), kind=kOutput, calls=%fused_computation.5.clone.1 | convolution fusion | flops 59899904 | bytes 3842049 | tf_op jit(solution)/shard_map/while/body/eval_jaxpr/ktjxab,jbd->ktxad/dot_general | solution.py:78
  101.0 13.1 %all-reduce = bf16[8,3,128]{2,1,0:T(4,128)(2,1)S(1)} all-reduce(bf16[8,3,128]{2,1,0:T(4,128)(2,1)S(1)} %bitcast.413), channel_id=3, replica_groups=mesh['sec'=4,'mom'=2,'en'=4] {'sec','mom'}, use_global_device_ids=true, to_apply=%region_10.11.clone | all-reduce | flops 3072 | bytes 12288
  114.6 10.7 %psum.7 = f32[1,3,128]{2,1,0:T(4,128)S(1)} all-reduce(f32[1,3,128]{2,1,0:T(4,128)S(1)} %dynamic-slice_convert_fusion), channel_id=1, replica_groups=mesh['sec'=4,'mom'=2,'en'=4] {'en'}, use_global_device_ids=true, to_apply=%region_11.12 | all-reduce | flops 384 | bytes 3072 | tf_op jit(solution)/shard_map/psum | solution.py:139
  125.8 1.7 %broadcast_multiply_fusion = f32[1,2,2,128,128]{4,3,2,1,0:T(8,128)} fusion(f32[1,2,2,128,128]{4,3,2,1,0:T(8,128)} %get-tuple-element.324), kind=kLoop, calls=%fused_computation.225 | loop fusion | flops 65536 | bytes 524288 | tf_op jit(solution)/shard_map/mul | solution.py:140
  (159 shorter events, 34.9 us)
Async XLA Ops:
  0.6 31.9 %copy-start = (s32[2,2]{1,0:T(2,128)S(1)}, s32[2,2]{1,0:T(2,128)}, u32[]{:S(2)}) copy-start(s32[2,2]{1,0:T(2,128)} %param.14) | copy-start | bytes 52
  0.6 8.8 %copy-start.16 = (s32[4]{0:T(128)S(1)}, s32[4]{0:T(128)}, u32[]{:S(2)}) copy-start(s32[4]{0:T(128)} %param.13) | copy-start | bytes 52
  0.7 32.4 %collective-permute-start = (bf16[1,2,2,128,128]{4,3,2,1,0:T(8,128)(2,1)}, bf16[1,2,2,128,128]{4,3,2,1,0:T(8,128)(2,1)S(1)}, u32[]{:S(2)}, u32[]{:S(2)}) collective-permute-start(bf16[1,2,2,128,128]{4,3,2,1,0:T(8,128)(2,1)} %param.9), channel_id=1, source_target_pairs={{0,1},{1,2},{2,3},{3,8},{8,9},{9,10},{10,11},{11,16},{16,17},{17,1... | collective-permute-start | bytes 393224 | tf_op jit(solution)/shard_map/ppermute | solution.py:12
  9.4 22.5 %copy-start.17 = (u32[32]{0:T(128)S(1)}, u32[32]{0:T(128)}, u32[]{:S(2)}) copy-start(u32[32]{0:T(128)} %constant.93) | copy-start | bytes 388
  9.4 23.6 %copy-start.14 = (bf16[1,2,2,128,128]{4,3,2,1,0:T(8,128)(2,1)S(1)}, bf16[1,2,2,128,128]{4,3,2,1,0:T(8,128)(2,1)}, u32[]{:S(2)}) copy-start(bf16[1,2,2,128,128]{4,3,2,1,0:T(8,128)(2,1)} %param.9) | copy-start | bytes 393220
  31.9 11.1 %copy-start.1 = (bf16[3,128,128]{2,1,0:T(8,128)(2,1)S(1)}, bf16[3,128,128]{2,1,0:T(8,128)(2,1)}, u32[]{:S(2)}) copy-start(bf16[3,128,128]{2,1,0:T(8,128)(2,1)} %param.10) | copy-start | bytes 294916
  63.4 1.4 %copy-start.5 = (f32[2,128,128]{2,1,0:T(8,128)S(1)}, f32[2,128,128]{2,1,0:T(8,128)}, u32[]{:S(2)}) copy-start(f32[2,128,128]{2,1,0:T(8,128)} %copy.221) | copy-start | bytes 393220 | tf_op jit(solution)/shard_map/while
  63.4 1.4 %copy-start.6 = (f32[2,128,128]{2,1,0:T(8,128)S(1)}, f32[2,128,128]{2,1,0:T(8,128)}, u32[]{:S(2)}) copy-start(f32[2,128,128]{2,1,0:T(8,128)} %copy.222) | copy-start | bytes 393220 | tf_op jit(solution)/shard_map/while
  63.4 1.4 %copy-start.7 = (f32[2,128,128]{2,1,0:T(8,128)S(1)}, f32[2,128,128]{2,1,0:T(8,128)}, u32[]{:S(2)}) copy-start(f32[2,128,128]{2,1,0:T(8,128)} %copy.223) | copy-start | bytes 393220 | tf_op jit(solution)/shard_map/while
  63.4 1.4 %copy-start.8 = (f32[2,128,128]{2,1,0:T(8,128)S(1)}, f32[2,128,128]{2,1,0:T(8,128)}, u32[]{:S(2)}) copy-start(f32[2,128,128]{2,1,0:T(8,128)} %copy.224) | copy-start | bytes 393220 | tf_op jit(solution)/shard_map/while
  63.4 1.4 %copy-start.9 = (f32[2,128,128]{2,1,0:T(8,128)S(1)}, f32[2,128,128]{2,1,0:T(8,128)}, u32[]{:S(2)}) copy-start(f32[2,128,128]{2,1,0:T(8,128)} %copy.225) | copy-start | bytes 393220 | tf_op jit(solution)/shard_map/while
  63.4 1.4 %copy-start.10 = (f32[2,128,128]{2,1,0:T(8,128)S(1)}, f32[2,128,128]{2,1,0:T(8,128)}, u32[]{:S(2)}) copy-start(f32[2,128,128]{2,1,0:T(8,128)} %copy.226) | copy-start | bytes 393220 | tf_op jit(solution)/shard_map/while
  63.5 1.4 %copy-start.11 = (f32[2,128,128]{2,1,0:T(8,128)S(1)}, f32[2,128,128]{2,1,0:T(8,128)}, u32[]{:S(2)}) copy-start(f32[2,128,128]{2,1,0:T(8,128)} %copy.227) | copy-start | bytes 393220 | tf_op jit(solution)/shard_map/while
  63.5 1.4 %copy-start.12 = (f32[2,128,128]{2,1,0:T(8,128)S(1)}, f32[2,128,128]{2,1,0:T(8,128)}, u32[]{:S(2)}) copy-start(f32[2,128,128]{2,1,0:T(8,128)} %copy.228) | copy-start | bytes 393220 | tf_op jit(solution)/shard_map/while
  63.5 1.4 %copy-start.13 = (f32[2,128,128]{2,1,0:T(8,128)S(1)}, f32[2,128,128]{2,1,0:T(8,128)}, u32[]{:S(2)}) copy-start(f32[2,128,128]{2,1,0:T(8,128)} %copy.204) | copy-start | bytes 393220 | tf_op jit(solution)/shard_map/while
  92.3 1.4 %copy-start.5 = (f32[2,128,128]{2,1,0:T(8,128)S(1)}, f32[2,128,128]{2,1,0:T(8,128)}, u32[]{:S(2)}) copy-start(f32[2,128,128]{2,1,0:T(8,128)} %copy.221) | copy-start | bytes 393220 | tf_op jit(solution)/shard_map/while
  92.3 1.4 %copy-start.6 = (f32[2,128,128]{2,1,0:T(8,128)S(1)}, f32[2,128,128]{2,1,0:T(8,128)}, u32[]{:S(2)}) copy-start(f32[2,128,128]{2,1,0:T(8,128)} %copy.222) | copy-start | bytes 393220 | tf_op jit(solution)/shard_map/while
  92.3 1.4 %copy-start.7 = (f32[2,128,128]{2,1,0:T(8,128)S(1)}, f32[2,128,128]{2,1,0:T(8,128)}, u32[]{:S(2)}) copy-start(f32[2,128,128]{2,1,0:T(8,128)} %copy.223) | copy-start | bytes 393220 | tf_op jit(solution)/shard_map/while
  92.3 1.4 %copy-start.8 = (f32[2,128,128]{2,1,0:T(8,128)S(1)}, f32[2,128,128]{2,1,0:T(8,128)}, u32[]{:S(2)}) copy-start(f32[2,128,128]{2,1,0:T(8,128)} %copy.224) | copy-start | bytes 393220 | tf_op jit(solution)/shard_map/while
  92.3 1.4 %copy-start.9 = (f32[2,128,128]{2,1,0:T(8,128)S(1)}, f32[2,128,128]{2,1,0:T(8,128)}, u32[]{:S(2)}) copy-start(f32[2,128,128]{2,1,0:T(8,128)} %copy.225) | copy-start | bytes 393220 | tf_op jit(solution)/shard_map/while
  92.3 1.4 %copy-start.10 = (f32[2,128,128]{2,1,0:T(8,128)S(1)}, f32[2,128,128]{2,1,0:T(8,128)}, u32[]{:S(2)}) copy-start(f32[2,128,128]{2,1,0:T(8,128)} %copy.226) | copy-start | bytes 393220 | tf_op jit(solution)/shard_map/while
  92.3 1.4 %copy-start.11 = (f32[2,128,128]{2,1,0:T(8,128)S(1)}, f32[2,128,128]{2,1,0:T(8,128)}, u32[]{:S(2)}) copy-start(f32[2,128,128]{2,1,0:T(8,128)} %copy.227) | copy-start | bytes 393220 | tf_op jit(solution)/shard_map/while
  92.3 1.4 %copy-start.12 = (f32[2,128,128]{2,1,0:T(8,128)S(1)}, f32[2,128,128]{2,1,0:T(8,128)}, u32[]{:S(2)}) copy-start(f32[2,128,128]{2,1,0:T(8,128)} %copy.228) | copy-start | bytes 393220 | tf_op jit(solution)/shard_map/while
  92.4 1.4 %copy-start.13 = (f32[2,128,128]{2,1,0:T(8,128)S(1)}, f32[2,128,128]{2,1,0:T(8,128)}, u32[]{:S(2)}) copy-start(f32[2,128,128]{2,1,0:T(8,128)} %copy.204) | copy-start | bytes 393220 | tf_op jit(solution)/shard_map/while
  (8 other events, 9.4 us)
where the time goes:
time: 129 us; the launch traced here: 128 us
  blocking collectives  49.5 us (38%)
  local copies, waits for them, and re-layouts  37 us (29%)
  matrix products  19.7 us (15%)
  other arithmetic  9.8 us (8%)
  between operations  5.97 us (5%)
  starting transfers between devices  4.94 us (4%)
    mul x48, local copies, waits for them, and re-layouts, weighted_rows(): term = factor[:, None, :, :, :, None] * slab[None, :, None, None, :, :]  28 us
    all_gather x1, blocking collectives, per_device(): gathered = lax.all_gather(stacked, ('sec', 'mom'), axis=0, tiled=True)  15.9 us
    dot_general x2, matrix products, point_terms(): jnp.einsum('ktjxab,jbd->ktxad', combined, derivative, preferred_element_t...  14 us
    unnamed x1, blocking collectives  13.1 us
    psum x1, blocking collectives, per_device(): lax.psum(shares, 'en').reshape(local_modes, points, 3, block_order)  10.7 us
    all_gather x1, blocking collectives, per_device(): pieces = lax.all_gather(travelling, 'mom', axis=0, tiled=True)  9.85 us
    ppermute x1, starting transfers between devices, passed_along(): return lax.ppermute(x, axis, pairs)  4.94 us
    dot_general x2, matrix products, one_point(): jnp.einsum('kq,qmxija->kmxija', onehot, phonon_table, precision=lax.Preci...  3.61 us
  transfers between devices with their start and end apart: 1, of which 0 were waited for; matrix products, arithmetic and copies ran while one was open for 5% of the time, Pallas kernels for 0%

commit v1 on v0

v1 whole, which is shorter than its diff:
```python
import functools
import math

import jax
import jax.numpy as jnp
from jax import lax
from jax.experimental import pallas as pl
from jax.experimental.pallas import tpu as pltpu
from jax.sharding import PartitionSpec as P

MESH = pl.DeviceIdType.MESH
STRIDE = 32


def kernel(
    sizes,
    scales,
    off_ref,
    mom_ref,
    g_ref,
    d_ref,
    bare_ref,
    prior_ref,
    sigma_ref,
    polar_ref,
    rim,
    near,
    phon,
    wbuf,
    mix,
    terms,
    psend,
    precv,
    bsend,
    brecv,
    rim_send,
    rim_recv,
    near_send,
    near_recv,
    phon_send,
    phon_recv,
    pol_send,
    pol_recv,
    sum_send,
    sum_recv,
):
    secs, points, ens, levels, modes, order = sizes
    sigma_scale, polar_scale = scales
    f32, bf16 = jnp.float32, jnp.bfloat16
    sec, mom, en = lax.axis_index("sec"), lax.axis_index("mom"), lax.axis_index("en")
    group = secs * points
    gid = sec * points + mom
    chain = sec * ens + en
    has_next = chain + 1 < secs * ens
    has_prev = chain > 0
    next_chain = lax.rem(chain + 1, secs * ens)
    prev_chain = lax.rem(chain + secs * ens - 1, secs * ens)

    def at_group(index):
        return {"sec": index // points, "mom": lax.rem(index, points), "en": en}

    def at_chain(index, m):
        return {"sec": index // ens, "mom": m, "en": lax.rem(index, ens)}

    def at_en(index):
        return {"sec": sec, "mom": mom, "en": index}

    barrier = pltpu.get_barrier_semaphore()
    for rel in range(1, group):
        pl.semaphore_signal(
            barrier, inc=1, device_id=at_group(lax.rem(gid + rel, group)), device_id_type=MESH
        )
    for rel in range(1, ens):
        pl.semaphore_signal(
            barrier, inc=1, device_id=at_en(lax.rem(en + rel, ens)), device_id_type=MESH
        )
    up = jnp.logical_and(has_next, en == ens - 1)
    down = jnp.logical_and(has_prev, en == 0)
    for r in range(points):
        m = lax.rem(mom + r, points)

        @pl.when(has_next if r else up)
        def _():
            pl.semaphore_signal(
                barrier, inc=1, device_id=at_chain(next_chain, m), device_id_type=MESH
            )

        @pl.when(has_prev if r else down)
        def _():
            pl.semaphore_signal(
                barrier, inc=1, device_id=at_chain(prev_chain, m), device_id_type=MESH
            )

    def product(former, latter):
        out = []
        for i in range(3):
            re = im = None
            for m in range(3):
                fr, fi = former[0][i][m : m + 1], former[1][i][m : m + 1]
                lr, li = latter[0][m], latter[1][m]
                tr, ti = fr * lr - fi * li, fr * li + fi * lr
                re = tr if re is None else re + tr
                im = ti if im is None else im + ti
            out.append((re, im))
        return [[o[0] for o in out], [o[1] for o in out]]

    bare = [[bare_ref[c, i] for i in range(3)] for c in range(2)]
    prior = [[prior_ref[c, i] for i in range(3)] for c in range(2)]
    full = product(product(bare, prior), bare)
    for c in range(2):
        for i in range(3):
            phon[gid, 9 * c + 3 * i : 9 * c + 3 * i + 3, :] = bare[c][i] + full[c][i]

    @pl.when(jnp.logical_not(has_prev))
    def _():
        rim[...] = jnp.zeros_like(rim)

    one = lambda flag: jnp.where(flag, 1, 0)
    pl.semaphore_wait(
        barrier,
        group
        + ens
        - 2
        + (points - 1) * (one(has_next) + one(has_prev))
        + one(up)
        + one(down),
    )

    def phon_copy(rel):
        return pltpu.make_async_remote_copy(
            src_ref=phon.at[gid],
            dst_ref=phon.at[gid],
            send_sem=phon_send.at[rel],
            recv_sem=phon_recv.at[rel],
            device_id=at_group(lax.rem(gid + rel, group)),
            device_id_type=MESH,
        )

    def rim_copy(r):
        return pltpu.make_async_remote_copy(
            src_ref=g_ref,
            dst_ref=rim.at[r],
            send_sem=rim_send.at[r],
            recv_sem=rim_recv.at[r],
            device_id=at_chain(next_chain, lax.rem(mom + points - r, points)),
            device_id_type=MESH,
        )

    def near_copy(r):
        return pltpu.make_async_remote_copy(
            src_ref=g_ref.at[pl.ds(0, levels - 1)],
            dst_ref=near.at[r],
            send_sem=near_send.at[r],
            recv_sem=near_recv.at[r],
            device_id=at_chain(chain, lax.rem(mom + points - r, points)),
            device_id_type=MESH,
        )

    for rel in range(1, group):
        phon_copy(rel).start()

    @pl.when(has_next)
    def _():
        for r in range(points - 1, -1, -1):
            rim_copy(r).start()

    for r in range(1, points):
        near_copy(r).start()

    d_f32 = [d_ref[i].astype(f32) for i in range(3)]
    d_side = jnp.concatenate([d_ref[i] for i in range(3)], axis=1)
    right = jnp.concatenate(
        [g_ref[e, c] if c == 0 else -g_ref[e, c] for e in range(levels) for c in range(2)], axis=0
    )

    for rel in range(1, group):
        phon_copy(rel).wait()

    is_off = [[(off_ref[w] == d + 1).astype(f32) for d in range(levels)] for w in range(modes)]
    is_mom = [
        [(mom_ref[mom, lax.rem(mom + r, points)] == q).astype(f32) for q in range(points)]
        for r in range(points)
    ]
    summed = [
        [
            sum(is_off[w][d] * phon[w * points + q] for w in range(modes))
            for q in range(points)
        ]
        for d in range(levels)
    ]
    for r in range(points):
        for d in range(levels):
            base = (r * levels + d) * STRIDE
            wbuf[base : base + 18, :] = sum(
                is_mom[r][q] * summed[d][q] for q in range(points)
            )
    per = order // STRIDE
    for r in range(points):
        for d in range(levels):
            slot = r * levels + d
            if slot % per == 0:
                turned = jnp.transpose(wbuf[slot * STRIDE : slot * STRIDE + order, :])
            base = (slot % per) * STRIDE
            left = (r * levels + d) * 2 * order
            for j in range(3):
                parts = []
                for c in range(2):
                    acc = None
                    for i in range(3):
                        col = base + 9 * c + 3 * i + j
                        term = turned[:, col : col + 1] * d_f32[i]
                        acc = term if acc is None else acc + term
                    parts.append(acc.astype(bf16))
                row = j * 2 * order
                mix[row : row + order, left : left + order] = parts[0]
                mix[row : row + order, left + order : left + 2 * order] = -parts[1]
                mix[row + order : row + 2 * order, left : left + order] = parts[1]
                mix[row + order : row + 2 * order, left + order : left + 2 * order] = parts[0]

    d_turned = [jnp.transpose(d_f32[i]) for i in range(3)]

    for r in range(1, points):
        near_copy(r).wait()

    @pl.when(has_next)
    def _():
        for r in range(points):
            rim_copy(r).wait_send()

    @pl.when(has_prev)
    def _():
        for r in range(points):
            rim_copy(r).wait_recv()

    def block(r, level, c):
        if level < 0:
            return rim[r, levels + level, c]
        return g_ref[level, c] if r == 0 else near[r, level, c]

    for r in range(points):
        for d in range(levels):
            slot = r * levels + d
            left = jnp.concatenate(
                [block(r, e - d - 1, c) for e in range(levels) for c in range(2)], axis=1
            )
            inner = jnp.dot(left, right, preferred_element_type=f32).astype(bf16)
            outer = jnp.dot(inner, d_side, preferred_element_type=f32)
            for i in range(3):
                terms[slot, i : i + 1, :] = jnp.sum(
                    outer[:, i * order : (i + 1) * order] * d_turned[i], axis=0, keepdims=True
                )
    for w in range(modes):
        by_point = [
            sum(is_off[w][d] * terms[r * levels + d] for d in range(levels))
            for r in range(points)
        ]
        for q in range(points):
            psend[w * points + q] = sum(is_mom[r][q] * by_point[r] for r in range(points))

    def pol_copy(rel):
        return pltpu.make_async_remote_copy(
            src_ref=psend.at[lax.rem(gid + rel, group)],
            dst_ref=precv.at[rel],
            send_sem=pol_send.at[rel],
            recv_sem=pol_recv.at[rel],
            device_id=at_group(lax.rem(gid + rel, group)),
            device_id_type=MESH,
        )

    def sum_copy(rel):
        return pltpu.make_async_remote_copy(
            src_ref=bsend,
            dst_ref=brecv.at[rel],
            send_sem=sum_send.at[rel],
            recv_sem=sum_recv.at[rel],
            device_id=at_en(lax.rem(en + rel, ens)),
            device_id_type=MESH,
        )

    for rel in range(1, group):
        pol_copy(rel).start()

    stacked = jnp.concatenate(
        [
            jnp.concatenate([block(r, e - d - 1, c) for e in range(levels)], axis=1)
            for r in range(points)
            for d in range(levels)
            for c in range(2)
        ],
        axis=0,
    )
    middle = jnp.dot(mix[...], stacked, preferred_element_type=f32).astype(bf16)

    for rel in range(1, group):
        pol_copy(rel).wait()
    share = psend[gid]
    for rel in range(1, group):
        share = share + precv[rel]
    bsend[...] = share
    for rel in range(1, ens):
        sum_copy(rel).start()

    d_down = jnp.concatenate([d_ref[j] for j in range(3)], axis=0)
    for e in range(levels):
        for x in range(2):
            lhs = jnp.concatenate(
                [
                    middle[
                        (2 * j + x) * order : (2 * j + x + 1) * order,
                        e * order : (e + 1) * order,
                    ]
                    for j in range(3)
                ],
                axis=1,
            )
            sigma_ref[e, x] = jnp.dot(lhs, d_down, preferred_element_type=f32) * sigma_scale

    for rel in range(1, ens):
        sum_copy(rel).wait()
    for rel in range(1, ens):
        share = share + brecv[rel]
    polar_ref[...] = share * polar_scale


def per_device(green_blocks, derivative, bare_phonon, prior_polar, offsets, momenta):
    secs, points, ens = (lax.axis_size(a) for a in ("sec", "mom", "en"))
    levels, order = green_blocks.shape[1], green_blocks.shape[-1]
    modes = offsets.shape[0]
    if green_blocks.shape[0] != 1 or bare_phonon.shape[:2] != (1, 1) or levels < 2:
        raise ValueError("unsupported placement")
    group = secs * points
    f32, bf16 = jnp.float32, jnp.bfloat16
    sizes = (secs, points, ens, levels, modes, order)
    scales = (
        1.0 / math.sqrt(9.0 * modes * points),
        1.0 / math.sqrt(float(points * levels * secs * ens * order)),
    )
    slots = points * levels
    wrows = -(-slots * STRIDE // order) * order
    vmem = pl.BlockSpec(memory_space=pltpu.VMEM)
    smem = pl.BlockSpec(memory_space=pltpu.SMEM)
    dma = pltpu.SemaphoreType.DMA
    sigma, polar = pl.pallas_call(
        functools.partial(kernel, sizes, scales),
        out_shape=(
            jax.ShapeDtypeStruct((levels, 2, order, order), f32),
            jax.ShapeDtypeStruct((3, order), f32),
        ),
        in_specs=[smem, smem, vmem, vmem, vmem, vmem],
        out_specs=(vmem, vmem),
        scratch_shapes=[
            pltpu.VMEM((points, levels, 2, order, order), bf16),
            pltpu.VMEM((points, levels - 1, 2, order, order), bf16),
            pltpu.VMEM((group, 18, order), f32),
            pltpu.VMEM((wrows, order), f32),
            pltpu.VMEM((6 * order, slots * 2 * order), bf16),
            pltpu.VMEM((slots, 3, order), f32),
            pltpu.VMEM((group, 3, order), f32),
            pltpu.VMEM((group, 3, order), f32),
            pltpu.VMEM((3, order), f32),
            pltpu.VMEM((ens, 3, order), f32),
            dma((points,)),
            dma((points,)),
            dma((points,)),
            dma((points,)),
            dma((group,)),
            dma((group,)),
            dma((group,)),
            dma((group,)),
            dma((ens,)),
            dma((ens,)),
        ],
        compiler_params=pltpu.CompilerParams(
            collective_id=0, has_side_effects=True, vmem_limit_bytes=40 * 1024 * 1024
        ),
        name="born_loop",
    )(
        offsets,
        momenta,
        green_blocks.reshape(green_blocks.shape[1:]),
        derivative,
        bare_phonon.reshape(bare_phonon.shape[2:]),
        prior_polar.reshape(prior_polar.shape[2:]),
    )
    return sigma[None], polar[None, None]


def solution(mesh):
    return jax.shard_map(
        per_device,
        mesh=mesh,
        in_specs=(
            P("mom", ("sec", "en"), None, None, None),
            P(),
            P("sec", "mom", None, None, None, None),
            P("sec", "mom", None, None, None, None),
            P(),
            P(),
        ),
        out_specs=(P("mom", ("sec", "en"), None, None, None), P("sec", "mom", None, None)),
        check_vma=False,
    )
```

time: 129 us -> 26.7 us (0.21)
  blocking collectives: 49.5 us -> 0 us
  local copies, waits for them, and re-layouts: 37 us -> 4.46 us
  Pallas kernels: 0 us -> 21.3 us
  matrix products: 19.7 us -> 0 us
  other arithmetic: 9.8 us -> 0 us
  between operations: 5.97 us -> 0.65 us
  starting transfers between devices: 4.94 us -> 0 us
    mul x48 -> x0, local copies, waits for them, and re-layouts: 28 us -> none  [weighted_rows(): term = factor[:, None, :, :, :, None] * slab[None, :, None, None, :, :]]
    all_gather x2 -> x0, blocking collectives: 25.7 us -> none  [the longest x1 15.9 us: per_device(): gathered = lax.all_gather(stacked, ('sec', 'mom'), axis=0, tiled=True)]
    pallas_call x0 -> x1, Pallas kernels: none -> 21.3 us  [per_device(): pl.pallas_call(functools.partial(kernel, sizes, scales), out_shape=(jax.S...]
    dot_general x7 -> x0, matrix products: 19.7 us -> none  [the longest x2 14 us: point_terms(): jnp.einsum('ktjxab,jbd->ktxad', combined, derivative, preferred_element_t...]
    unnamed x1 -> x0, blocking collectives: 13.1 us -> none
    psum x1 -> x0, blocking collectives: 10.7 us -> none  [per_device(): lax.psum(shares, 'en').reshape(local_modes, points, 3, block_order)]
    ppermute x1 -> x0, starting transfers between devices: 4.94 us -> none  [passed_along(): return lax.ppermute(x, axis, pairs)]
    mul x12 -> x0, other arithmetic: 4.87 us -> none  [the longest x10 3.19 us: weighted_rows(): term = factor[:, None, :, :, :, None] * slab[None, :, None, None, :, :]]
  transfers between devices with their start and end apart: 1 -> 0, of which waited for: 0 -> 0; matrix products, arithmetic and copies ran while one was open for 5% -> 0% of each run, Pallas kernels for 0% -> 0%
where the time goes in v1:
time: 26.7 us; the launch traced here: 26.4 us
  Pallas kernels  21.3 us (80%)
  local copies, waits for them, and re-layouts  4.46 us (17%)
  between operations  0.65 us (2%)
    pallas_call x1, Pallas kernels, per_device(): pl.pallas_call(functools.partial(kernel, sizes, scales), out_shape=(jax.S...  21.3 us
    unnamed x10, local copies, waits for them, and re-layouts  3.73 us
    reshape x1, local copies, waits for them, and re-layouts, per_device(): prior_polar.reshape(prior_polar.shape[2:])  0.73 us

profile of v1, /device:TPU:0, one launch (start us, length us, event | category | flops | bytes accessed | tf_op | source)
XLA Modules:
  0.0 26.4 jit_solution(7403558130805951410)
XLA Ops:
  0.6 0.7 %copy_bitcast_fusion = (f32[2,3,3,128]{3,2,1,0:T(4,128)S(1)}, f32[2,3,3,128]{3,2,1,0:T(4,128)S(1)}) fusion(f32[1,1,2,3,3,128]{5,2,4,3,1,0:T(2,128)} %param.9, f32[1,1,2,3,3,128]{5,2,4,3,1,0:T(2,128)} %param.8), kind=kLoop, calls=%fused_computation | loop fusion | bytes 36864 | tf_op jit(solution)/shard_map/reshape | solution.py:383
  1.4 0.0 copy-start.2
  1.4 0.0 copy-start.3
  1.4 0.7 %copy-done.2 = s32[2,2]{1,0:T(2,128)S(1)} copy-done((s32[2,2]{1,0:T(2,128)S(1)}, s32[2,2]{1,0:T(2,128)}, u32[]{:S(2)}) %copy-start.2) | copy-done | bytes 40
  2.0 0.0 copy-done.3
  2.0 0.0 copy-start
  2.0 0.9 %copy-done = bf16[1,2,2,128,128]{4,3,2,1,0:T(8,128)(2,1)S(1)} copy-done((bf16[1,2,2,128,128]{4,3,2,1,0:T(8,128)(2,1)S(1)}, bf16[1,2,2,128,128]{4,3,2,1,0:T(8,128)(2,1)}, u32[]{:S(2)}) %copy-start) | copy-done | bytes 131096
  2.9 0.0 copy-start.1
  2.9 0.9 %copy-done.1 = bf16[3,128,128]{2,1,0:T(8,128)(2,1)S(1)} copy-done((bf16[3,128,128]{2,1,0:T(8,128)(2,1)S(1)}, bf16[3,128,128]{2,1,0:T(8,128)(2,1)}, u32[]{:S(2)}) %copy-start.1) | copy-done | bytes 98328
  3.8 21.3 %born_loop.1 = (f32[2,2,128,128]{3,2,1,0:T(8,128)S(1)}, f32[3,128]{1,0:T(4,128)S(1)}) custom-call(s32[4]{0:T(128)S(1)} %copy-done.3, s32[2,2]{1,0:T(2,128)S(1)} %copy-done.2, bf16[2,2,128,128]{3,2,1,0:T(8,128)(2,1)S(1)} %bitcast.8, bf16[3,128,128]{2,1,0:T(8,128)(2,1)S(1)} %copy-done.1, f32[2,3,3,128]{3,2,1,0:T(4,128)S(1)} %get-tuple-element.9.bare_ref, ...), custom_call_target="tpu_custom_call" | custom-call | tf_op jit(solution)/shard_map/born_loop/pallas_call | solution.py:343
  25.2 0.6 %copy.10 = f32[1,1,3,128]{3,1,2,0:T(1,128)} copy(f32[1,1,3,128]{3,2,1,0:T(4,128)S(1)} %bitcast.9) | data formatting | bytes 3072
  25.7 0.7 %copy.14 = f32[1,2,2,128,128]{4,3,2,1,0:T(8,128)} copy(f32[1,2,2,128,128]{4,3,2,1,0:T(8,128)S(1)} %bitcast.7) | data formatting | bytes 524288
Async XLA Ops:
  1.4 0.7 %copy-start.2 = (s32[2,2]{1,0:T(2,128)S(1)}, s32[2,2]{1,0:T(2,128)}, u32[]{:S(2)}) copy-start(s32[2,2]{1,0:T(2,128)} %mom_ref.1) | copy-start | bytes 52
  1.4 0.7 %copy-start.3 = (s32[4]{0:T(128)S(1)}, s32[4]{0:T(128)}, u32[]{:S(2)}) copy-start(s32[4]{0:T(128)} %off_ref.1) | copy-start | bytes 52
  2.0 0.9 %copy-start = (bf16[1,2,2,128,128]{4,3,2,1,0:T(8,128)(2,1)S(1)}, bf16[1,2,2,128,128]{4,3,2,1,0:T(8,128)(2,1)}, u32[]{:S(2)}) copy-start(bf16[1,2,2,128,128]{4,3,2,1,0:T(8,128)(2,1)} %param.6) | copy-start | bytes 393220
  2.9 0.9 %copy-start.1 = (bf16[3,128,128]{2,1,0:T(8,128)(2,1)S(1)}, bf16[3,128,128]{2,1,0:T(8,128)(2,1)}, u32[]{:S(2)}) copy-start(bf16[3,128,128]{2,1,0:T(8,128)(2,1)} %d_ref.1) | copy-start | bytes 294916

commit v2 on v1

v2 whole, which is shorter than its diff:
```python
import functools
import math

import jax
import jax.numpy as jnp
from jax import lax
from jax.experimental import pallas as pl
from jax.experimental.pallas import tpu as pltpu
from jax.sharding import PartitionSpec as P

MESH = pl.DeviceIdType.MESH
STRIDE = 32


def kernel(
    sizes,
    scales,
    off_in,
    mom_in,
    g_in,
    d_in,
    bare_in,
    prior_in,
    sigma_ref,
    polar_ref,
    off_ref,
    mom_ref,
    g_ref,
    d_ref,
    bare_ref,
    prior_ref,
    rim,
    near,
    phon,
    wbuf,
    mix,
    terms,
    psend,
    precv,
    load_sem,
    rim_send,
    rim_recv,
    near_send,
    near_recv,
    phon_send,
    phon_recv,
    pol_send,
    pol_recv,
):
    secs, points, ens, levels, modes, order = sizes
    sigma_scale, polar_scale = scales
    f32, bf16 = jnp.float32, jnp.bfloat16
    sec, mom, en = lax.axis_index("sec"), lax.axis_index("mom"), lax.axis_index("en")
    group = secs * points
    gid = sec * points + mom
    chain = sec * ens + en
    has_next = chain + 1 < secs * ens
    has_prev = chain > 0
    next_chain = lax.rem(chain + 1, secs * ens)
    prev_chain = lax.rem(chain + secs * ens - 1, secs * ens)

    def at_group(index):
        return {"sec": index // points, "mom": lax.rem(index, points), "en": en}

    def at_chain(index, m):
        return {"sec": index // ens, "mom": m, "en": lax.rem(index, ens)}

    def at_en(index):
        return {"sec": sec, "mom": mom, "en": index}

    loads = [
        pltpu.make_async_copy(src, dst, load_sem.at[n])
        for n, (src, dst) in enumerate(
            [
                (bare_in, bare_ref),
                (prior_in, prior_ref),
                (off_in, off_ref),
                (mom_in, mom_ref),
                (g_in, g_ref),
                (d_in, d_ref),
            ]
        )
    ]
    for load in loads:
        load.start()

    total = group * ens
    me = gid * ens + en

    def everywhere(body):
        if total <= 64:
            for rel in range(1, total):
                body(rel)
        else:
            lax.fori_loop(1, total, lambda rel, _: (body(rel), 0)[1], 0)

    def at_rel(rel):
        index = lax.rem(me + rel, total)
        return {
            "sec": index // (points * ens),
            "mom": lax.rem(index // ens, points),
            "en": lax.rem(index, ens),
        }

    barrier = pltpu.get_barrier_semaphore()

    def greet(rel):
        pl.semaphore_signal(barrier, inc=1, device_id=at_rel(rel), device_id_type=MESH)

    everywhere(greet)

    for load in loads:
        load.wait()

    def product(former, latter):
        out = []
        for i in range(3):
            re = im = None
            for m in range(3):
                fr, fi = former[0][i][m : m + 1], former[1][i][m : m + 1]
                lr, li = latter[0][m], latter[1][m]
                tr, ti = fr * lr - fi * li, fr * li + fi * lr
                re = tr if re is None else re + tr
                im = ti if im is None else im + ti
            out.append((re, im))
        return [[o[0] for o in out], [o[1] for o in out]]

    bare = [[bare_ref[i, :, c, :] for i in range(3)] for c in range(2)]
    prior = [[prior_ref[i, :, c, :] for i in range(3)] for c in range(2)]
    full = product(product(bare, prior), bare)
    for c in range(2):
        for i in range(3):
            phon[gid, 9 * c + 3 * i : 9 * c + 3 * i + 3, :] = bare[c][i] + full[c][i]

    @pl.when(jnp.logical_not(has_prev))
    def _():
        rim[...] = jnp.zeros_like(rim)

    pl.semaphore_wait(barrier, total - 1)

    def phon_copy(rel):
        return pltpu.make_async_remote_copy(
            src_ref=phon.at[gid],
            dst_ref=phon.at[gid],
            send_sem=phon_send.at[rel],
            recv_sem=phon_recv.at[rel],
            device_id=at_group(lax.rem(gid + rel, group)),
            device_id_type=MESH,
        )

    def rim_copy(r):
        return pltpu.make_async_remote_copy(
            src_ref=g_ref,
            dst_ref=rim.at[r],
            send_sem=rim_send.at[r],
            recv_sem=rim_recv.at[r],
            device_id=at_chain(next_chain, lax.rem(mom + points - r, points)),
            device_id_type=MESH,
        )

    def near_copy(r):
        return pltpu.make_async_remote_copy(
            src_ref=g_ref.at[pl.ds(0, levels - 1)],
            dst_ref=near.at[r],
            send_sem=near_send.at[r],
            recv_sem=near_recv.at[r],
            device_id=at_chain(chain, lax.rem(mom + points - r, points)),
            device_id_type=MESH,
        )

    @pl.when(has_next)
    def _():
        for r in range(points - 1, -1, -1):
            rim_copy(r).start()

    for r in range(1, points):
        near_copy(r).start()

    for rel in range(1, group):
        phon_copy(rel).start()

    d_f32 = [d_ref[i].astype(f32) for i in range(3)]
    d_side = jnp.concatenate([d_ref[i] for i in range(3)], axis=1)
    right = jnp.concatenate(
        [g_ref[e, c] if c == 0 else -g_ref[e, c] for e in range(levels) for c in range(2)], axis=0
    )

    is_off = [[(off_ref[w] == d + 1).astype(f32) for d in range(levels)] for w in range(modes)]
    is_mom = [
        [(mom_ref[mom, lax.rem(mom + r, points)] == q).astype(f32) for q in range(points)]
        for r in range(points)
    ]
    d_turned = [jnp.transpose(d_f32[i]) for i in range(3)]

    for r in range(1, points):
        near_copy(r).wait()

    @pl.when(has_next)
    def _():
        for r in range(points):
            rim_copy(r).wait_send()

    @pl.when(has_prev)
    def _():
        for r in range(points):
            rim_copy(r).wait_recv()

    def block(r, level, c):
        if level < 0:
            return rim[r, levels + level, c]
        return g_ref[level, c] if r == 0 else near[r, level, c]

    for r in range(points):
        for d in range(levels):
            slot = r * levels + d
            left = jnp.concatenate(
                [block(r, e - d - 1, c) for e in range(levels) for c in range(2)], axis=1
            )
            inner = jnp.dot(left, right, preferred_element_type=f32).astype(bf16)
            outer = jnp.dot(inner, d_side, preferred_element_type=f32)
            for i in range(3):
                terms[slot, i : i + 1, :] = jnp.sum(
                    outer[:, i * order : (i + 1) * order] * d_turned[i], axis=0, keepdims=True
                )
    for w in range(modes):
        by_point = [
            sum(is_off[w][d] * terms[r * levels + d] for d in range(levels))
            for r in range(points)
        ]
        for q in range(points):
            psend[w * points + q] = sum(is_mom[r][q] * by_point[r] for r in range(points))

    def pol_copy(rel):
        return pltpu.make_async_remote_copy(
            src_ref=psend.at[lax.rem(me + rel, total) // ens],
            dst_ref=precv.at[rel],
            send_sem=pol_send.at[rel],
            recv_sem=pol_recv.at[rel],
            device_id=at_rel(rel),
            device_id_type=MESH,
        )

    everywhere(lambda rel: pol_copy(rel).start())

    for rel in range(1, group):
        phon_copy(rel).wait()

    summed = [
        [
            sum(is_off[w][d] * phon[w * points + q] for w in range(modes))
            for q in range(points)
        ]
        for d in range(levels)
    ]
    for r in range(points):
        for d in range(levels):
            base = (r * levels + d) * STRIDE
            wbuf[base : base + 18, :] = sum(
                is_mom[r][q] * summed[d][q] for q in range(points)
            )
    per = order // STRIDE
    for r in range(points):
        for d in range(levels):
            slot = r * levels + d
            if slot % per == 0:
                turned = jnp.transpose(wbuf[slot * STRIDE : slot * STRIDE + order, :])
            base = (slot % per) * STRIDE
            left = (r * levels + d) * 2 * order
            for j in range(3):
                parts = []
                for c in range(2):
                    acc = None
                    for i in range(3):
                        col = base + 9 * c + 3 * i + j
                        term = turned[:, col : col + 1] * d_f32[i]
                        acc = term if acc is None else acc + term
                    parts.append(acc.astype(bf16))
                row = j * 2 * order
                mix[row : row + order, left : left + order] = parts[0]
                mix[row : row + order, left + order : left + 2 * order] = -parts[1]
                mix[row + order : row + 2 * order, left : left + order] = parts[1]
                mix[row + order : row + 2 * order, left + order : left + 2 * order] = parts[0]

    stacked = jnp.concatenate(
        [
            jnp.concatenate([block(r, e - d - 1, c) for e in range(levels)], axis=1)
            for r in range(points)
            for d in range(levels)
            for c in range(2)
        ],
        axis=0,
    )
    middle = jnp.dot(mix[...], stacked, preferred_element_type=f32).astype(bf16)

    d_down = jnp.concatenate([d_ref[j] for j in range(3)], axis=0)
    for e in range(levels):
        for x in range(2):
            lhs = jnp.concatenate(
                [
                    middle[
                        (2 * j + x) * order : (2 * j + x + 1) * order,
                        e * order : (e + 1) * order,
                    ]
                    for j in range(3)
                ],
                axis=1,
            )
            sigma_ref[e, x] = jnp.dot(lhs, d_down, preferred_element_type=f32) * sigma_scale

    everywhere(lambda rel: pol_copy(rel).wait())
    precv[0] = psend[gid]
    share = jnp.sum(precv[...], axis=0)
    polar_ref[:, 0, :] = share * polar_scale


def per_device(green_blocks, derivative, bare_phonon, prior_polar, offsets, momenta):
    secs, points, ens = (lax.axis_size(a) for a in ("sec", "mom", "en"))
    levels, order = green_blocks.shape[1], green_blocks.shape[-1]
    modes = offsets.shape[0]
    if green_blocks.shape[0] != 1 or bare_phonon.shape[:2] != (1, 1) or levels < 2:
        raise ValueError("unsupported placement")
    group = secs * points
    f32, bf16 = jnp.float32, jnp.bfloat16
    sizes = (secs, points, ens, levels, modes, order)
    scales = (
        1.0 / math.sqrt(9.0 * modes * points),
        1.0 / math.sqrt(float(points * levels * secs * ens * order)),
    )
    slots = points * levels
    wrows = -(-slots * STRIDE // order) * order
    vmem = pl.BlockSpec(memory_space=pltpu.VMEM)
    hbm = pl.BlockSpec(memory_space=pltpu.HBM)
    dma = pltpu.SemaphoreType.DMA
    sigma, polar = pl.pallas_call(
        functools.partial(kernel, sizes, scales),
        out_shape=(
            jax.ShapeDtypeStruct((levels, 2, order, order), f32),
            jax.ShapeDtypeStruct((3, 1, order), f32),
        ),
        in_specs=[hbm] * 6,
        out_specs=(vmem, vmem),
        scratch_shapes=[
            pltpu.SMEM(offsets.shape, jnp.int32),
            pltpu.SMEM(momenta.shape, jnp.int32),
            pltpu.VMEM((levels, 2, order, order), bf16),
            pltpu.VMEM(derivative.shape, bf16),
            pltpu.VMEM((3, 3, 2, order), f32),
            pltpu.VMEM((3, 3, 2, order), f32),
            pltpu.VMEM((points, levels, 2, order, order), bf16),
            pltpu.VMEM((points, levels - 1, 2, order, order), bf16),
            pltpu.VMEM((group, 18, order), f32),
            pltpu.VMEM((wrows, order), f32),
            pltpu.VMEM((6 * order, slots * 2 * order), bf16),
            pltpu.VMEM((slots, 3, order), f32),
            pltpu.VMEM((group, 3, order), f32),
            pltpu.VMEM((group * ens, 3, order), f32),
            dma((6,)),
            dma((points,)),
            dma((points,)),
            dma((points,)),
            dma((points,)),
            dma((group,)),
            dma((group,)),
            dma((group * ens,)),
            dma((group * ens,)),
        ],
        compiler_params=pltpu.CompilerParams(
            collective_id=0, has_side_effects=True, vmem_limit_bytes=64 * 1024 * 1024 - 65536
        ),
        name="born_loop",
    )(
        offsets,
        momenta,
        green_blocks.reshape(green_blocks.shape[1:]),
        derivative,
        jnp.transpose(bare_phonon[0, 0], (1, 2, 0, 3)),
        jnp.transpose(prior_polar[0, 0], (1, 2, 0, 3)),
    )
    return sigma[None], polar.reshape(1, 1, 3, order)


def solution(mesh):
    return jax.shard_map(
        per_device,
        mesh=mesh,
        in_specs=(
            P("mom", ("sec", "en"), None, None, None),
            P(),
            P("sec", "mom", None, None, None, None),
            P("sec", "mom", None, None, None, None),
            P(),
            P(),
        ),
        out_specs=(P("mom", ("sec", "en"), None, None, None), P("sec", "mom", None, None)),
        check_vma=False,
    )
```

time: 26.7 us -> 23.6 us (0.88)
  local copies, waits for them, and re-layouts: 4.46 us -> 2.24 us
  Pallas kernels: 21.3 us -> 20.6 us
    unnamed x10 -> x4, local copies, waits for them, and re-layouts: 3.73 us -> 2.24 us
    pallas_call x1, Pallas kernels: 21.3 us -> 20.6 us  [per_device(): pl.pallas_call(functools.partial(kernel, sizes, scales), out_shape=(jax.S...]
    reshape x1 -> x0, local copies, waits for them, and re-layouts: 0.73 us -> none  [per_device(): prior_polar.reshape(prior_polar.shape[2:])]
where the time goes in v2:
time: 23.6 us; the launch traced here: 23.4 us
  Pallas kernels  20.6 us (87%)
  local copies, waits for them, and re-layouts  2.24 us (9%)
  between operations  0.65 us (3%)
    pallas_call x1, Pallas kernels, per_device(): pl.pallas_call(functools.partial(kernel, sizes, scales), out_shape=(jax.S...  20.6 us
    unnamed x4, local copies, waits for them, and re-layouts  2.24 us

profile of v2, /device:TPU:0, one launch (start us, length us, event | category | flops | bytes accessed | tf_op | source)
XLA Modules:
  0.0 23.4 jit_solution(15104873464615088651)
XLA Ops:
  0.6 20.6 %born_loop.1 = (f32[2,2,128,128]{3,2,1,0:T(8,128)}, f32[3,1,128]{2,1,0:T(1,128)}) custom-call(s32[4]{0:T(128)} %off_in.1, s32[2,2]{1,0:T(2,128)} %mom_in.1, bf16[2,2,128,128]{3,2,1,0:T(8,128)(2,1)} %bitcast.12, bf16[3,128,128]{2,1,0:T(8,128)(2,1)} %d_in.1, f32[3,3,2,128]{3,2,1,0:T(2,128)} %bitcast.13, f32[3,3,2,128]{3,2,1,0:T(2,128)} %bitcast.14), custom_call_target="tpu_custom_call" | custom-call | tf_op jit(solution)/shard_map/born_loop/pallas_call | solution.py:334
  21.2 0.0 copy-start
  21.2 1.7 %copy.11 = f32[1,2,2,128,128]{4,3,2,1,0:T(8,128)} copy(f32[1,2,2,128,128]{4,3,2,1,0:T(8,128)} %bitcast.11) | data formatting | bytes 524288
  22.9 0.0 copy-done
  22.9 0.6 %copy.12 = f32[1,1,3,128]{3,1,2,0:T(1,128)} copy(f32[1,1,3,128]{3,1,2,0:T(1,128)S(1)} %bitcast.15) | data formatting | bytes 3072
Async XLA Ops:
  21.2 1.7 %copy-start = (f32[3,1,128]{2,1,0:T(1,128)S(1)}, f32[3,1,128]{2,1,0:T(1,128)}, u32[]{:S(2)}) copy-start(f32[3,1,128]{2,1,0:T(1,128)} %get-tuple-element.5) | copy-start | bytes 4612

commit v3 on v2

--- a/solution.py
+++ b/solution.py
@@ -14,7 +14,6 @@
 
 def kernel(
     sizes,
-    scales,
     off_in,
     mom_in,
     g_in,
@@ -48,7 +47,6 @@
     pol_recv,
 ):
     secs, points, ens, levels, modes, order = sizes
-    sigma_scale, polar_scale = scales
     f32, bf16 = jnp.float32, jnp.bfloat16
     sec, mom, en = lax.axis_index("sec"), lax.axis_index("mom"), lax.axis_index("en")
     group = secs * points
@@ -234,8 +232,8 @@
         return pltpu.make_async_remote_copy(
             src_ref=psend.at[lax.rem(me + rel, total) // ens],
             dst_ref=precv.at[rel],
-            send_sem=pol_send.at[rel],
-            recv_sem=pol_recv.at[rel],
+            send_sem=pol_send,
+            recv_sem=pol_recv,
             device_id=at_rel(rel),
             device_id_type=MESH,
         )
@@ -305,12 +303,14 @@
                 ],
                 axis=1,
             )
-            sigma_ref[e, x] = jnp.dot(lhs, d_down, preferred_element_type=f32) * sigma_scale
-
-    everywhere(lambda rel: pol_copy(rel).wait())
+            sigma_ref[e, x] = jnp.dot(lhs, d_down, preferred_element_type=f32)
+
+    rest = precv.at[pl.ds(1, total - 1)]
+    for sem in (pol_send, pol_recv):
+        pltpu.make_async_copy(rest, rest, sem).wait()
     precv[0] = psend[gid]
     share = jnp.sum(precv[...], axis=0)
-    polar_ref[:, 0, :] = share * polar_scale
+    polar_ref[:, 0, :] = share
 
 
 def per_device(green_blocks, derivative, bare_phonon, prior_polar, offsets, momenta):
@@ -332,7 +332,7 @@
     hbm = pl.BlockSpec(memory_space=pltpu.HBM)
     dma = pltpu.SemaphoreType.DMA
     sigma, polar = pl.pallas_call(
-        functools.partial(kernel, sizes, scales),
+        functools.partial(kernel, sizes),
         out_shape=(
             jax.ShapeDtypeStruct((levels, 2, order, order), f32),
             jax.ShapeDtypeStruct((3, 1, order), f32),
@@ -361,8 +361,8 @@
             dma((points,)),
             dma((group,)),
             dma((group,)),
-            dma((group * ens,)),
-            dma((group * ens,)),
+            dma,
+            dma,
         ],
         compiler_params=pltpu.CompilerParams(
             collective_id=0, has_side_effects=True, vmem_limit_bytes=64 * 1024 * 1024 - 65536
@@ -376,7 +376,7 @@
         jnp.transpose(bare_phonon[0, 0], (1, 2, 0, 3)),
         jnp.transpose(prior_polar[0, 0], (1, 2, 0, 3)),
     )
-    return sigma[None], polar.reshape(1, 1, 3, order)
+    return sigma[None] * scales[0], polar.reshape(1, 1, 3, order) * scales[1]
 
 
 def solution(mesh):

time: 23.6 us -> 23.1 us (0.979)
  other arithmetic: 0 us -> 2.24 us
  local copies, waits for them, and re-layouts: 2.24 us -> 0.01 us
  Pallas kernels: 20.6 us -> 20 us
    unnamed x4 -> x2, local copies, waits for them, and re-layouts: 2.24 us -> 0.01 us
    mul x0 -> x1, other arithmetic: none -> 1.68 us  [per_device(): return (sigma[None] * scales[0], polar.reshape(1, 1, 3, order) * scales[1])]
    pallas_call x1, Pallas kernels: 20.6 us -> 20 us  [per_device(): pl.pallas_call(functools.partial(kernel, sizes), out_shape=(jax.ShapeDtyp...]
    unnamed x0 -> x1, other arithmetic: none -> 0.56 us
where the time goes in v3:
time: 23.1 us; the launch traced here: 22.9 us
  Pallas kernels  20 us (87%)
  other arithmetic  2.24 us (10%)
  between operations  0.65 us (3%)
    pallas_call x1, Pallas kernels, per_device(): pl.pallas_call(functools.partial(kernel, sizes), out_shape=(jax.ShapeDtyp...  20 us
    mul x1, other arithmetic, per_device(): return (sigma[None] * scales[0], polar.reshape(1, 1, 3, order) * scales[1])  1.68 us
    unnamed x1, other arithmetic  0.56 us

profile of v3, /device:TPU:0, one launch (start us, length us, event | category | flops | bytes accessed | tf_op | source)
XLA Modules:
  0.0 22.9 jit_solution(6359662295783542048)
XLA Ops:
  0.6 20.0 %born_loop.1 = (f32[2,2,128,128]{3,2,1,0:T(8,128)}, f32[3,1,128]{2,1,0:T(1,128)}) custom-call(s32[4]{0:T(128)} %off_in.1, s32[2,2]{1,0:T(2,128)} %mom_in.1, bf16[2,2,128,128]{3,2,1,0:T(8,128)(2,1)} %bitcast.13, bf16[3,128,128]{2,1,0:T(8,128)(2,1)} %d_in.1, f32[3,3,2,128]{3,2,1,0:T(2,128)} %bitcast.14, f32[3,3,2,128]{3,2,1,0:T(2,128)} %bitcast.15), custom_call_target="tpu_custom_call" | custom-call | tf_op jit(solution)/shard_map/born_loop/pallas_call | solution.py:334
  20.6 0.0 copy-start
  20.6 1.7 %multiply_bitcast_fusion = f32[1,2,2,128,128]{4,3,2,1,0:T(8,128)} fusion(f32[2,2,128,128]{3,2,1,0:T(8,128)} %get-tuple-element.4), kind=kLoop, calls=%fused_computation | loop fusion | flops 65536 | bytes 524288 | tf_op jit(solution)/shard_map/mul | solution.py:379
  22.3 0.0 copy-done
  22.3 0.6 %multiply_bitcast_fusion.1 = f32[1,1,3,128]{3,1,2,0:T(1,128)} fusion(f32[3,1,128]{2,1,0:T(1,128)S(1)} %copy-done), kind=kLoop, calls=%fused_computation.1 | loop fusion | flops 384 | bytes 3072
Async XLA Ops:
  20.6 1.7 %copy-start = (f32[3,1,128]{2,1,0:T(1,128)S(1)}, f32[3,1,128]{2,1,0:T(1,128)}, u32[]{:S(2)}) copy-start(f32[3,1,128]{2,1,0:T(1,128)} %get-tuple-element.5) | copy-start | bytes 4612

commit v4 on v3

--- a/solution.py
+++ b/solution.py
@@ -57,14 +57,8 @@
     next_chain = lax.rem(chain + 1, secs * ens)
     prev_chain = lax.rem(chain + secs * ens - 1, secs * ens)
 
-    def at_group(index):
-        return {"sec": index // points, "mom": lax.rem(index, points), "en": en}
-
     def at_chain(index, m):
         return {"sec": index // ens, "mom": m, "en": lax.rem(index, ens)}
-
-    def at_en(index):
-        return {"sec": sec, "mom": mom, "en": index}
 
     loads = [
         pltpu.make_async_copy(src, dst, load_sem.at[n])
@@ -83,22 +77,25 @@
         load.start()
 
     total = group * ens
-    me = gid * ens + en
+    sec_at = [sec] + [lax.rem(sec + k, secs) for k in range(1, secs)]
+    mom_at = [mom] + [lax.rem(mom + k, points) for k in range(1, points)]
+    en_at = [en] + [lax.rem(en + k, ens) for k in range(1, ens)]
+    row_at = [[a * points + b for b in mom_at] for a in sec_at]
 
     def everywhere(body):
-        if total <= 64:
-            for rel in range(1, total):
-                body(rel)
-        else:
-            lax.fori_loop(1, total, lambda rel, _: (body(rel), 0)[1], 0)
+        for rel in range(1, total):
+            body(rel)
+
+    def split(rel):
+        return rel // (points * ens), rel // ens % points, rel % ens
 
     def at_rel(rel):
-        index = lax.rem(me + rel, total)
-        return {
-            "sec": index // (points * ens),
-            "mom": lax.rem(index // ens, points),
-            "en": lax.rem(index, ens),
-        }
+        a, b, c = split(rel)
+        return {"sec": sec_at[a], "mom": mom_at[b], "en": en_at[c]}
+
+    def row_of(rel):
+        a, b, _ = split(rel)
+        return row_at[a][b]
 
     barrier = pltpu.get_barrier_semaphore()
 
@@ -142,7 +139,7 @@
             dst_ref=phon.at[gid],
             send_sem=phon_send.at[rel],
             recv_sem=phon_recv.at[rel],
-            device_id=at_group(lax.rem(gid + rel, group)),
+            device_id=at_rel(rel * ens),
             device_id_type=MESH,
         )
 
@@ -230,7 +227,7 @@
 
     def pol_copy(rel):
         return pltpu.make_async_remote_copy(
-            src_ref=psend.at[lax.rem(me + rel, total) // ens],
+            src_ref=psend.at[row_of(rel)],
             dst_ref=precv.at[rel],
             send_sem=pol_send,
             recv_sem=pol_recv,

time: 23.1 us -> 22.7 us (0.983)
  Pallas kernels: 20 us -> 19.6 us
    pallas_call x1, Pallas kernels: 20 us -> 19.6 us  [per_device(): pl.pallas_call(functools.partial(kernel, sizes), out_shape=(jax.ShapeDtyp...]
where the time goes in v4:
time: 22.7 us; the launch traced here: 22.5 us
  Pallas kernels  19.6 us (86%)
  other arithmetic  2.24 us (10%)
  between operations  0.65 us (3%)
    pallas_call x1, Pallas kernels, per_device(): pl.pallas_call(functools.partial(kernel, sizes), out_shape=(jax.ShapeDtyp...  19.6 us
    mul x1, other arithmetic, per_device(): return (sigma[None] * scales[0], polar.reshape(1, 1, 3, order) * scales[1])  1.68 us
    unnamed x1, other arithmetic  0.56 us

profile of v4, /device:TPU:0, one launch (start us, length us, event | category | flops | bytes accessed | tf_op | source)
XLA Modules:
  0.0 22.5 jit_solution(1927922533263556102)
XLA Ops:
  0.6 19.6 %born_loop.1 = (f32[2,2,128,128]{3,2,1,0:T(8,128)}, f32[3,1,128]{2,1,0:T(1,128)}) custom-call(s32[4]{0:T(128)} %off_in.1, s32[2,2]{1,0:T(2,128)} %mom_in.1, bf16[2,2,128,128]{3,2,1,0:T(8,128)(2,1)} %bitcast.13, bf16[3,128,128]{2,1,0:T(8,128)(2,1)} %d_in.1, f32[3,3,2,128]{3,2,1,0:T(2,128)} %bitcast.14, f32[3,3,2,128]{3,2,1,0:T(2,128)} %bitcast.15), custom_call_target="tpu_custom_call" | custom-call | tf_op jit(solution)/shard_map/born_loop/pallas_call | solution.py:331
  20.2 0.0 copy-start
  20.2 1.7 %multiply_bitcast_fusion = f32[1,2,2,128,128]{4,3,2,1,0:T(8,128)} fusion(f32[2,2,128,128]{3,2,1,0:T(8,128)} %get-tuple-element.4), kind=kLoop, calls=%fused_computation | loop fusion | flops 65536 | bytes 524288 | tf_op jit(solution)/shard_map/mul | solution.py:376
  21.9 0.0 copy-done
  21.9 0.6 %multiply_bitcast_fusion.1 = f32[1,1,3,128]{3,1,2,0:T(1,128)} fusion(f32[3,1,128]{2,1,0:T(1,128)S(1)} %copy-done), kind=kLoop, calls=%fused_computation.1 | loop fusion | flops 384 | bytes 3072
Async XLA Ops:
  20.2 1.7 %copy-start = (f32[3,1,128]{2,1,0:T(1,128)S(1)}, f32[3,1,128]{2,1,0:T(1,128)}, u32[]{:S(2)}) copy-start(f32[3,1,128]{2,1,0:T(1,128)} %get-tuple-element.5) | copy-start | bytes 4612
